TPU v7x, 32 devices: a whole 2x2x4 slice. The times are simulated.
32 devices in a mesh: dp: 16 (over z, y, core), tensor: 2 (over x).
Axes of the slice: x: 2, y: 2, z: 4, core: 2. Of those that a mesh axis runs over, the one named last changes fastest.
Arguments:
- tokens: bfloat16 [32768, 1024], P(('dp', 'tensor')), may hold values from -6 to 6
- doc_lengths: int32 [32, 4], P('dp'), may hold values from 1 to 800, 1024 in all within a row
- ln1_gain: bfloat16 [1024], replicated, may hold values from 0.099609375 to 1.8984375
- ln1_bias: bfloat16 [1024], replicated, may hold values from -1.5 to 1.5
- w_query: bfloat16 [1024, 1024], P('dp', 'tensor'), may hold values from -0.1875 to 0.1875
- b_query: bfloat16 [1024], P('tensor'), may hold values from -2.5 to 2.5
- w_key: bfloat16 [1024, 1024], P('dp', 'tensor'), may hold values from -0.1875 to 0.1875
- w_value: bfloat16 [1024, 1024], P('dp', 'tensor'), may hold values from -0.1875 to 0.1875
- b_value: bfloat16 [1024], P('tensor'), may hold values from -2.5 to 2.5
- w_dense: bfloat16 [1024, 1024], P('tensor', 'dp'), may hold values from -0.5 to 0.5
- b_dense: bfloat16 [1024], replicated, may hold values from -2.5 to 2.5
- ln2_gain: bfloat16 [1024], replicated, may hold values from 0.099609375 to 1.8984375
- ln2_bias: bfloat16 [1024], replicated, may hold values from -1.5 to 1.5
- w_up: bfloat16 [1024, 4096], P('dp', 'tensor'), may hold values from -0.1875 to 0.1875
- b_up: bfloat16 [4096], P('tensor'), may hold values from -2.5 to 2.5
- w_down: bfloat16 [4096, 1024], P('tensor', 'dp'), may hold values from -0.125 to 0.125
- b_down: bfloat16 [1024], replicated, may hold values from -2.5 to 2.5
- out_grad: bfloat16 [32768, 1024], P(('dp', 'tensor')), may hold values from -6 to 6
Outputs:
- mixed: bfloat16 [32768, 1024], P(('dp', 'tensor'))
- tokens_grad: bfloat16 [32768, 1024], P(('dp', 'tensor'))
- ln1_gain_grad: float32 [1024], replicated
- ln1_bias_grad: float32 [1024], replicated
- w_query_grad: float32 [1024, 1024], P('dp', 'tensor')
- b_query_grad: float32 [1024], P('tensor')
- w_key_grad: float32 [1024, 1024], P('dp', 'tensor')
- w_value_grad: float32 [1024, 1024], P('dp', 'tensor')
- b_value_grad: float32 [1024], P('tensor')
- w_dense_grad: float32 [1024, 1024], P('tensor', 'dp')
- b_dense_grad: float32 [1024], replicated
- ln2_gain_grad: float32 [1024], replicated
- ln2_bias_grad: float32 [1024], replicated
- w_up_grad: float32 [1024, 4096], P('dp', 'tensor')
- b_up_grad: float32 [4096], P('tensor')
- w_down_grad: float32 [4096, 1024], P('tensor', 'dp')
- b_down_grad: float32 [1024], replicated
Inputs may be any that keep to these rules, and one draw needn't show every extreme that they name: `doc_lengths`: each row holds the lengths of the 4 documents of one sequence in order; they sum to 1024, and each row's longest is exactly 800.
All inputs are finite; a program needn't handle non-finite values.
Results may differ from a plain program's by a relative error of at most 0.018.
Values may be sent and summed in bfloat16 or wider, within the bound.
A program may use at most 192 MiB of HBM per device.

v0:
```python
import jax
import jax.numpy as jnp
from jax import lax
from jax.sharding import PartitionSpec as P

HEADS = 16
HDIM = 64
SEQ_LEN = 1024


epsilon = 1e-05


def normalize(field, norm_gain, norm_shift):
    average = jnp.mean(field, -1, keepdims=True)
    centred = field - average
    factor = lax.rsqrt(jnp.mean(centred * centred, -1, keepdims=True) + epsilon)
    normed = centred * factor
    return (normed * norm_gain + norm_shift, normed, factor)


def norm_back(upstream, normed, factor, norm_gain):
    scaled = upstream * norm_gain
    return factor * (
        scaled
        - jnp.mean(scaled, -1, keepdims=True)
        - normed * jnp.mean(scaled * normed, -1, keepdims=True)
    )


def gelu_tanh(field):
    return jax.nn.gelu(field, approximate=True)


def block_scores(query_rows, keys_all, segment_ids, slopes, offset):
    rows_here = query_rows.shape[0]
    length = keys_all.shape[0]
    factor = query_rows.shape[2] ** (-0.5)
    query_place = offset + jnp.arange(rows_here, dtype=jnp.int32)
    key_place = jnp.arange(length, dtype=jnp.int32)
    distance = (key_place[None, :] - query_place[:, None]).astype(jnp.float32)
    query_segment = segment_ids[offset : offset + rows_here]
    allowed = (key_place[None, :] <= query_place[:, None]) & (
        segment_ids[None, :] == query_segment[:, None]
    )
    scores = (
        jnp.einsum("qhd,khd->hqk", query_rows, keys_all, preferred_element_type=jnp.float32)
        * factor
    )
    scores = scores + slopes[:, None, None] * distance[None]
    return jnp.where(allowed[None], scores, -1e30)


def attend_forward(query, keys_all, values_all, segment_ids, slopes):
    length = query.shape[0]
    span = min(512, length)
    outputs = []
    totals = []
    for offset in range(0, length, span):
        scores = block_scores(query[offset : offset + span], keys_all, segment_ids, slopes, offset)
        row_max = jnp.max(scores, -1, keepdims=True)
        raised = jnp.exp(scores - row_max)
        row_sum = jnp.sum(raised, -1, keepdims=True)
        attn_probs = (raised / row_sum).astype(jnp.bfloat16)
        outputs.append(
            jnp.einsum("hqk,khd->qhd", attn_probs, values_all, preferred_element_type=jnp.float32)
        )
        totals.append((row_max + jnp.log(row_sum))[:, :, 0])
    return (jnp.concatenate(outputs, 0).astype(jnp.bfloat16), jnp.concatenate(totals, 1))


def attend_backward(query, keys_all, values_all, segment_ids, slopes, out_grads, log_totals):
    length = query.shape[0]
    span = min(512, length)
    factor = query.shape[2] ** (-0.5)
    query_grads = []
    key_grad = jnp.zeros(keys_all.shape, jnp.float32)
    value_grad = jnp.zeros(values_all.shape, jnp.float32)
    for offset in range(0, length, span):
        query_rows = query[offset : offset + span]
        grad_rows = out_grads[offset : offset + span]
        scores = block_scores(query_rows, keys_all, segment_ids, slopes, offset)
        attn_probs = jnp.exp(scores - log_totals[:, offset : offset + span, None])
        value_grad = value_grad + jnp.einsum(
            "hqk,qhd->khd",
            attn_probs.astype(jnp.bfloat16),
            grad_rows,
            preferred_element_type=jnp.float32,
        )
        prob_grads = jnp.einsum(
            "qhd,khd->hqk", grad_rows, values_all, preferred_element_type=jnp.float32
        )
        score_grads = (
            attn_probs * (prob_grads - jnp.sum(attn_probs * prob_grads, -1, keepdims=True))
        ).astype(jnp.bfloat16)
        query_grads.append(
            jnp.einsum("hqk,khd->qhd", score_grads, keys_all, preferred_element_type=jnp.float32)
            * factor
        )
        key_grad = (
            key_grad
            + jnp.einsum(
                "hqk,qhd->khd", score_grads, query_rows, preferred_element_type=jnp.float32
            )
            * factor
        )
    return (
        jnp.concatenate(query_grads, 0).astype(jnp.bfloat16),
        key_grad.astype(jnp.bfloat16),
        value_grad.astype(jnp.bfloat16),
    )


def shards(
    tokens,
    doc_lengths,
    ln1_gain,
    ln1_bias,
    w_query,
    b_query,
    w_key,
    w_value,
    b_value,
    w_dense,
    b_dense,
    ln2_gain,
    ln2_bias,
    w_up,
    b_up,
    w_down,
    b_down,
    out_grad,
):
    shard_set = (w_query, w_key, w_value, w_dense, w_up, w_down)
    query_w, key_w, value_w, dense_w, up_w, down_w = (
        lax.all_gather(shard_set[0], "dp", axis=0, tiled=True),
        lax.all_gather(shard_set[1], "dp", axis=0, tiled=True),
        lax.all_gather(shard_set[2], "dp", axis=0, tiled=True),
        lax.all_gather(shard_set[3], "dp", axis=1, tiled=True),
        lax.all_gather(shard_set[4], "dp", axis=0, tiled=True),
        lax.all_gather(shard_set[5], "dp", axis=1, tiled=True),
    )
    local_heads = query_w.shape[1] // HDIM
    first_head = lax.axis_index("tensor") * local_heads
    head_number = first_head + jnp.arange(local_heads, dtype=jnp.int32) + 1
    slopes = 2.0 ** (-8.0 * head_number.astype(jnp.float32) / HEADS)
    seq_count = doc_lengths.shape[0]
    doc_ends = jnp.cumsum(doc_lengths, axis=1)
    places = jnp.arange(SEQ_LEN, dtype=jnp.int32)
    segment_ids = jnp.sum((places[None, :, None] >= doc_ends[:, None, :]).astype(jnp.int32), axis=2)
    own_rows = tokens.shape[0]
    field = tokens.astype(jnp.float32)
    gain_one = ln1_gain.astype(jnp.float32)
    shift_one = ln1_bias.astype(jnp.float32)
    gain_two = ln2_gain.astype(jnp.float32)
    shift_two = ln2_bias.astype(jnp.float32)
    out_one, normed_one, factor_one = normalize(field, gain_one, shift_one)
    norm_rows = lax.all_gather(out_one.astype(jnp.bfloat16), "tensor", axis=0, tiled=True)
    query = (
        jnp.dot(norm_rows, query_w, preferred_element_type=jnp.float32)
        + b_query.astype(jnp.float32)
    ).astype(jnp.bfloat16)
    keys_all = jnp.dot(norm_rows, key_w, preferred_element_type=jnp.float32).astype(jnp.bfloat16)
    values_all = (
        jnp.dot(norm_rows, value_w, preferred_element_type=jnp.float32)
        + b_value.astype(jnp.float32)
    ).astype(jnp.bfloat16)
    split_shape = (seq_count, SEQ_LEN, local_heads, HDIM)
    query_split = query.reshape(split_shape)
    keys_split = keys_all.reshape(split_shape)
    values_split = values_all.reshape(split_shape)

    def forward_one(members):
        return attend_forward(members[0], members[1], members[2], members[3], slopes)

    context, log_totals = lax.map(forward_one, (query_split, keys_split, values_split, segment_ids))
    context = context.reshape(query.shape)
    hidden_one = (
        field
        + lax.psum_scatter(
            jnp.dot(
                lax.slice_in_dim(context, 0, own_rows * lax.axis_size("tensor"), axis=0),
                dense_w,
                preferred_element_type=jnp.float32,
            ),
            "tensor",
            scatter_dimension=0,
            tiled=True,
        )
        + b_dense.astype(jnp.float32)
    )
    out_two, normed_two, factor_two = normalize(hidden_one, gain_two, shift_two)
    mlp_rows = lax.all_gather(out_two.astype(jnp.bfloat16), "tensor", axis=0, tiled=True)
    up_field = jnp.dot(mlp_rows, up_w, preferred_element_type=jnp.float32) + b_up.astype(
        jnp.float32
    )
    gelu_field, gelu_pull = jax.vjp(gelu_tanh, up_field)
    activated = gelu_field.astype(jnp.bfloat16)
    branch_sum = lax.psum_scatter(
        jnp.dot(
            lax.slice_in_dim(activated, 0, lax.axis_size("tensor") * own_rows, axis=0),
            down_w,
            preferred_element_type=jnp.float32,
        ).astype(jnp.bfloat16),
        "tensor",
        scatter_dimension=0,
        tiled=True,
    ).astype(jnp.float32)
    mixed_field = hidden_one + branch_sum + b_down.astype(jnp.float32)
    mixed = mixed_field.astype(jnp.bfloat16)
    query_w, key_w, value_w, dense_w, up_w, down_w = (
        lax.all_gather(shard_set[0], "dp", axis=0, tiled=True),
        lax.all_gather(shard_set[1], "dp", axis=0, tiled=True),
        lax.all_gather(shard_set[2], "dp", axis=0, tiled=True),
        lax.all_gather(shard_set[3], "dp", axis=1, tiled=True),
        lax.all_gather(shard_set[4], "dp", axis=0, tiled=True),
        lax.all_gather(shard_set[5], "dp", axis=1, tiled=True),
    )
    grad_rows = lax.all_gather(out_grad, "tensor", axis=0, tiled=True)
    act_grad = jnp.einsum("td,fd->tf", grad_rows, down_w, preferred_element_type=jnp.float32)
    up_grad = gelu_pull(act_grad)[0].astype(jnp.bfloat16)
    down_w_grad = jnp.einsum("tf,td->fd", activated, grad_rows, preferred_element_type=jnp.float32)
    up_w_grad = jnp.einsum("td,tf->df", mlp_rows, up_grad, preferred_element_type=jnp.float32)
    up_b_grad = jnp.sum(up_grad.astype(jnp.float32), 0)
    norm_two_grad = lax.psum_scatter(
        jnp.einsum(
            "tf,df->td",
            lax.slice_in_dim(up_grad, 0, own_rows * lax.axis_size("tensor"), axis=0),
            up_w,
            preferred_element_type=jnp.float32,
        ),
        "tensor",
        scatter_dimension=0,
        tiled=True,
    )
    outer_grad = out_grad.astype(jnp.float32)
    hidden_grad = outer_grad + norm_back(norm_two_grad, normed_two, factor_two, gain_two)
    gain_two_grad = jnp.sum(norm_two_grad * normed_two, 0)
    shift_two_grad = jnp.sum(norm_two_grad, 0)
    down_b_grad = jnp.sum(outer_grad, 0)
    dense_b_grad = jnp.sum(hidden_grad, 0)
    branch_rows = lax.all_gather(hidden_grad.astype(jnp.bfloat16), "tensor", axis=0, tiled=True)
    context_grad = jnp.einsum(
        "td,cd->tc", branch_rows, dense_w, preferred_element_type=jnp.float32
    ).astype(jnp.bfloat16)
    dense_w_grad = jnp.einsum("tc,td->cd", context, branch_rows, preferred_element_type=jnp.float32)

    def backward_one(members):
        return attend_backward(
            members[0], members[1], members[2], members[3], slopes, members[4], members[5]
        )

    query_grad, key_grad, value_grad = lax.map(
        backward_one,
        (
            query_split,
            keys_split,
            values_split,
            segment_ids,
            context_grad.reshape(split_shape),
            log_totals,
        ),
    )
    query_grad = query_grad.reshape(query.shape)
    key_grad = key_grad.reshape(query.shape)
    value_grad = value_grad.reshape(query.shape)
    query_w_grad = jnp.einsum(
        "td,tc->dc", norm_rows, query_grad, preferred_element_type=jnp.float32
    )
    key_w_grad = jnp.einsum("td,tc->dc", norm_rows, key_grad, preferred_element_type=jnp.float32)
    value_w_grad = jnp.einsum(
        "td,tc->dc", norm_rows, value_grad, preferred_element_type=jnp.float32
    )
    query_b_grad = jnp.sum(query_grad.astype(jnp.float32), 0)
    value_b_grad = jnp.sum(value_grad.astype(jnp.float32), 0)
    part_query = lax.slice_in_dim(query_grad, 0, own_rows * lax.axis_size("tensor"), axis=0)
    part_key = lax.slice_in_dim(key_grad, 0, own_rows * lax.axis_size("tensor"), axis=0)
    part_value = lax.slice_in_dim(value_grad, 0, own_rows * lax.axis_size("tensor"), axis=0)
    norm_one_grad = lax.psum_scatter(
        jnp.einsum("tc,dc->td", part_query, query_w, preferred_element_type=jnp.float32)
        + jnp.einsum("tc,dc->td", part_key, key_w, preferred_element_type=jnp.float32)
        + jnp.einsum("tc,dc->td", part_value, value_w, preferred_element_type=jnp.float32),
        "tensor",
        scatter_dimension=0,
        tiled=True,
    )
    tokens_grad = (hidden_grad + norm_back(norm_one_grad, normed_one, factor_one, gain_one)).astype(
        jnp.bfloat16
    )
    gain_one_grad = jnp.sum(norm_one_grad * normed_one, 0)
    shift_one_grad = jnp.sum(norm_one_grad, 0)
    query_w_sum, key_w_sum, value_w_sum, dense_w_sum, up_w_sum, down_w_sum = (
        lax.psum_scatter(
            query_w_grad.astype(jnp.bfloat16), "dp", scatter_dimension=0, tiled=True
        ).astype(jnp.float32),
        lax.psum_scatter(
            key_w_grad.astype(jnp.bfloat16), "dp", scatter_dimension=0, tiled=True
        ).astype(jnp.float32),
        lax.psum_scatter(
            value_w_grad.astype(jnp.bfloat16), "dp", scatter_dimension=0, tiled=True
        ).astype(jnp.float32),
        lax.psum_scatter(
            dense_w_grad.astype(jnp.bfloat16), "dp", scatter_dimension=1, tiled=True
        ).astype(jnp.float32),
        lax.psum_scatter(
            up_w_grad.astype(jnp.bfloat16), "dp", scatter_dimension=0, tiled=True
        ).astype(jnp.float32),
        lax.psum_scatter(
            down_w_grad.astype(jnp.bfloat16), "dp", scatter_dimension=1, tiled=True
        ).astype(jnp.float32),
    )
    query_b_sum, value_b_sum, up_b_sum = lax.psum((query_b_grad, value_b_grad, up_b_grad), "dp")
    gain_one_sum, shift_one_sum, dense_b_sum, gain_two_sum, shift_two_sum, down_b_sum = lax.psum(
        (gain_one_grad, shift_one_grad, dense_b_grad, gain_two_grad, shift_two_grad, down_b_grad),
        ("dp", "tensor"),
    )
    return (
        mixed,
        tokens_grad,
        gain_one_sum,
        shift_one_sum,
        query_w_sum,
        query_b_sum,
        key_w_sum,
        value_w_sum,
        value_b_sum,
        dense_w_sum,
        dense_b_sum,
        gain_two_sum,
        shift_two_sum,
        up_w_sum,
        up_b_sum,
        down_w_sum,
        down_b_sum,
    )


def solution(mesh):
    placed = (
        P(("dp", "tensor"), None),
        P("dp", None),
        P(),
        P(),
        P("dp", "tensor"),
        P("tensor"),
        P("dp", "tensor"),
        P("dp", "tensor"),
        P("tensor"),
        P("tensor", "dp"),
        P(),
        P(),
        P(),
        P("dp", "tensor"),
        P("tensor"),
        P("tensor", "dp"),
        P(),
        P(("dp", "tensor"), None),
    )
    return jax.shard_map(
        shards,
        mesh=mesh,
        in_specs=placed,
        out_specs=(
            P(("dp", "tensor"), None),
            P(("dp", "tensor"), None),
            P(),
            P(),
            P("dp", "tensor"),
            P("tensor"),
            P("dp", "tensor"),
            P("dp", "tensor"),
            P("tensor"),
            P("tensor", "dp"),
            P(),
            P(),
            P(),
            P("dp", "tensor"),
            P("tensor"),
            P("tensor", "dp"),
            P(),
        ),
        check_vma=False,
    )
```

profile of v0, /device:TPU:0, one launch (start us, length us, event | category | flops | bytes accessed | tf_op | source)
XLA Modules:
  0.0 1457.8 jit_solution(7123500544896009650)
XLA Ops:
  18.7 32.2 %all-gather.13.cloned.1.call-done = bf16[1024,512]{1,0:T(8,128)(2,1)} async-done(((bf16[64,512]{1,0:T(8,128)(2,1)}), bf16[1024,512]{1,0:T(8,128)(2,1)}) %all-gather.13.cloned.1.call-update) | async-done | bytes 1048592 | tf_op jit(solution)/shard_map/all_gather | solution.py:138
  50.9 57.8 %all-gather.11.cloned.1.call-done = bf16[2048,1024]{1,0:T(8,128)(2,1)} async-done(((bf16[1024,1024]{1,0:T(8,128)(2,1)}), bf16[2048,1024]{1,0:T(8,128)(2,1)}) %all-gather.11.cloned.1.call-update) | async-done | bytes 4194320 | tf_op jit(solution)/shard_map/all_gather | solution.py:158
  108.7 4.8 add_convert_fusion.4
  117.1 5.5 copy.60
  122.6 26.2 %all-gather.15.cloned.1.call-done = bf16[1024,512]{1,0:T(8,128)(2,1)} async-done(((bf16[64,512]{1,0:T(8,128)(2,1)}), bf16[1024,512]{1,0:T(8,128)(2,1)}) %all-gather.15.cloned.1.call-update) | async-done | bytes 1048592 | tf_op jit(solution)/shard_map/all_gather | solution.py:136
  148.8 4.8 add_convert_fusion.3
  157.2 5.5 copy.61
  162.7 25.0 %all-gather.17.cloned.1.call-done = bf16[1024,512]{1,0:T(8,128)(2,1)} async-done(((bf16[64,512]{1,0:T(8,128)(2,1)}), bf16[1024,512]{1,0:T(8,128)(2,1)}) %all-gather.17.cloned.1.call-update) | async-done | bytes 1048592 | tf_op jit(solution)/shard_map/all_gather | solution.py:137
  187.7 4.8 convolution_convert_fusion.4
  196.2 4.5 copy.62
  202.2 61.7 %while.28 = (s32[]{:T(128)}, bf16[2,1024,8,64]{1,3,2,0:T(8,128)(2,1)}, f32[2,8,1024]{2,1,0:T(8,128)}, bf16[2,1024,8,64]{1,3,2,0:T(8,128)(2,1)}, s32[2,1024]{1,0:...) while((s32[]{:T(128)}, ...), condition=%wide.region_9.10_spmd.clone, body=%wide.region_4.9_spmd.clone.sunk | while | flops 2239234560 | bytes 153454384 | solution.py:176
  205.5 4.6 fusion.180
  217.4 6.1 fusion.183
  236.1 4.6 fusion.180
  248.1 6.1 fusion.183
  263.9 4.5 copy.63
  270.4 7.5 fusion.102
  278.8 97.5 %reduce-scatter.11.cloned.1.call-done = f32[1024,1024]{1,0:T(8,128)} async-done(((f32[2048,1024]{1,0:T(8,128)}), f32[1024,1024]{1,0:T(8,128)}) %reduce-scatter.11.cloned.1.call-update) | async-done | bytes 4194320 | tf_op jit(solution)/shard_map/reduce_scatter | solution.py:180
  384.6 44.6 %all-gather.23.cloned.1.call-done = bf16[1024,2048]{1,0:T(8,128)(2,1)} async-done(((bf16[64,2048]{1,0:T(8,128)(2,1)}), bf16[1024,2048]{1,0:T(8,128)(2,1)}) %all-gather.23.cloned.1.call-update) | async-done | bytes 4194320 | tf_op jit(solution)/shard_map/all_gather | solution.py:140
  429.3 57.5 %all-gather.21.cloned.1.call-done = bf16[2048,1024]{1,0:T(8,128)(2,1)} async-done(((bf16[1024,1024]{1,0:T(8,128)(2,1)}), bf16[2048,1024]{1,0:T(8,128)(2,1)}) %all-gather.21.cloned.1.call-update) | async-done | bytes 4194320 | tf_op jit(solution)/shard_map/all_gather | solution.py:193
  486.8 15.6 %fusion.103 = f32[2048,2048]{1,0:T(8,128)} fusion(bf16[2048,1024]{1,0:T(8,128)(2,1)} %all-gather.21.cloned.1.call-done, bf16[1024,2048]{1,0:T(8,128)(2,1)} %all-gather.23.cloned.1.call-done), kind=kOutput, calls=%fused_computation.178 | convolution fusion | flops 8589934592 | bytes 25165824 | tf_op jit(solution)/shard_map/dot_general | solution.py:194
  502.3 42.8 %all-gather.27.cloned.1.call-done = bf16[2048,1024]{1,0:T(8,128)(2,1)} async-done(((bf16[1024,1024]{1,0:T(8,128)(2,1)}), bf16[2048,1024]{1,0:T(8,128)(2,1)}) %all-gather.27.cloned.1.call-update) | async-done | bytes 4194320 | tf_op jit(solution)/shard_map/all_gather | solution.py:219
  545.2 52.8 %all-gather.25.cloned.1.call-done = bf16[2048,1024]{0,1:T(8,128)(2,1)} async-done(((bf16[2048,64]{0,1:T(8,128)(2,1)}), bf16[2048,1024]{0,1:T(8,128)(2,1)}) %all-gather.25.cloned.1.call-update) | async-done | bytes 4194320 | tf_op jit(solution)/shard_map/all_gather | solution.py:141
  598.0 26.7 %convert_reduce_fusion = (f32[2048]{0:T(1024)}, bf16[2048,2048]{1,0:T(8,128)(2,1)S(1)}, bf16[2048,2048]{1,0:T(8,128)(2,1)}) fusion(f32[2048,2048]{1,0:T(8,128)} %fusion.103, f32[2048]{0:T(1024)S(1)} %convert_element_type.214, bf16[2048,1024]{1,0:T(8,128)(2,1)} %all-gather.27.cloned.1.call-done, bf16[2048,1024]{0,1:T(8,128)(2,1)} %all-gather.25.cloned.1.call-done), kind=kOutput, calls=%fused_computation.117 | convolution fusion | flops 8694790144 | bytes 41959424 | tf_op jit(solution)/shard_map/td,fd->tf/dot_general | solution.py:220
  627.9 11.6 fusion.104
  639.7 13.9 convolution_convert_fusion.1
  654.2 83.2 %reduce-scatter.15.cloned.1.call-done = f32[1024,1024]{1,0:T(8,128)} async-done(((f32[2048,1024]{1,0:T(8,128)}), f32[1024,1024]{1,0:T(8,128)}) %reduce-scatter.15.cloned.1.call-update) | async-done | bytes 4194320 | tf_op jit(solution)/shard_map/reduce_scatter | solution.py:225
  737.5 5.0 multiply_reduce_fusion.2
  742.5 51.5 %reduce-scatter.13.cloned.1.call-done = bf16[1024,1024]{1,0:T(8,128)(2,1)} async-done(((bf16[2048,1024]{1,0:T(8,128)(2,1)}), bf16[1024,1024]{1,0:T(8,128)(2,1)}) %reduce-scatter.13.cloned.1.call-update) | async-done | bytes 2097168 | tf_op jit(solution)/shard_map/reduce_scatter | solution.py:199
  794.0 6.7 fusion.96
  804.4 14.3 convolution_convert_fusion
  818.8 14.0 convolution_convert_fusion.2
  832.9 28.4 %all-gather.29.cloned.1.call-done = bf16[2048,1024]{1,0:T(8,128)(2,1)} async-done(((bf16[1024,1024]{1,0:T(8,128)(2,1)}), bf16[2048,1024]{1,0:T(8,128)(2,1)}) %all-gather.29.cloned.1.call-update) | async-done | bytes 4194320 | tf_op jit(solution)/shard_map/all_gather | solution.py:242
  861.3 4.5 convolution_convert_fusion.3
  865.8 4.0 reshape.474
  869.9 5.9 copy.67
  875.8 5.8 convolution_convert_fusion.5
  886.5 227.2 %while.29 = (s32[]{:T(128)}, bf16[2,1024,8,64]{1,3,2,0:T(8,128)(2,1)}, bf16[2,1024,8,64]{1,3,2,0:T(8,128)(2,1)}, bf16[2,1024,8,64]{1,3,2,0:T(8,128)(2,1)}, bf16[...) while((s32[]{:T(128)}, ...), condition=%wide.region_20.21_spmd.clone, body=%wide.region_17.20_spmd.clone.sunk | while | flops 5471986176 | bytes 559160512 | solution.py:253
  891.3 9.2 fusion.197
  900.4 13.7 multiply_reduce_fusion.9
  914.1 11.8 multiply_convert_fusion.6
  929.9 4.3 fusion.205
  937.7 9.3 fusion.201
  947.0 14.1 multiply_reduce_fusion.10
  961.2 15.5 %multiply_convert_fusion.7 = bf16[8,512,1024]{2,1,0:T(8,128)(2,1)} fusion(f32[8,512,1024]{2,1,0:T(8,128)} %get-tuple-element.465, f32[8,512,1024]{2,1,0:T(8,128)} %fusion.201, f32[8,512]{1,0:T(8,128)S(1)} %get-tuple-element.466), kind=kLoop, calls=%fused_computation.48.clone.1 | loop fusion | flops 12582912 | bytes 41959424 | tf_op jit(solution)/shard_map/while/body/eval_jaxpr/convert_element_type | solution.py:95
  984.4 6.4 fusion.202
  990.8 5.2 fusion.203
  1005.3 9.2 fusion.197
  1014.4 13.7 multiply_reduce_fusion.9
  1028.1 11.8 multiply_convert_fusion.6
  1043.9 4.3 fusion.205
  1051.7 9.3 fusion.201
  1061.0 13.7 multiply_reduce_fusion.10
  1074.7 15.0 %multiply_convert_fusion.7 = bf16[8,512,1024]{2,1,0:T(8,128)(2,1)} fusion(f32[8,512,1024]{2,1,0:T(8,128)} %get-tuple-element.465, f32[8,512,1024]{2,1,0:T(8,128)} %fusion.201, f32[8,512]{1,0:T(8,128)S(1)} %get-tuple-element.466), kind=kLoop, calls=%fused_computation.48.clone.1 | loop fusion | flops 12582912 | bytes 41959424 | tf_op jit(solution)/shard_map/while/body/eval_jaxpr/convert_element_type | solution.py:95
  1097.4 6.2 fusion.202
  1103.6 5.1 fusion.203
  1138.9 4.5 fusion.106
  1145.8 5.8 add_add_fusion
  1159.5 61.5 %all-reduce.1 = (f32[512]{0:T(512)}, f32[512]{0:T(512)}, f32[2048]{0:T(1024)}) all-reduce(f32[512]{0:T(512)S(1)} %reduce_sum.214, f32[512]{0:T(512)S(1)} %reduce_sum.216, f32[2048]{0:T(1024)S(1)} %copy-done.44), channel_id=1, replica_groups=mesh['dp'=16,'tensor'=2] {'dp'}, use_global_device_ids=true, to_apply=%region_30.31 | all-reduce | flops 3072 | bytes 24576 | tf_op jit(solution)/shard_map/psum | solution.py:312
  1224.0 17.1 %reduce-scatter.23.cloned.1.call-done = bf16[64,512]{1,0:T(8,128)(2,1)} async-done(((bf16[1024,512]{1,0:T(8,128)(2,1)}), bf16[64,512]{1,0:T(8,128)(2,1)}) %reduce-scatter.23.cloned.1.call-update) | async-done | bytes 65552 | tf_op jit(solution)/shard_map/reduce_scatter | solution.py:299
  1242.6 58.6 %reduce-scatter.21.cloned.1.call-done = bf16[64,512]{1,0:T(8,128)(2,1)} async-done(((bf16[1024,512]{1,0:T(8,128)(2,1)}), bf16[64,512]{1,0:T(8,128)(2,1)}) %reduce-scatter.21.cloned.1.call-update) | async-done | bytes 65552 | tf_op jit(solution)/shard_map/reduce_scatter | solution.py:296
  1302.7 99.0 %reduce-scatter.17.cloned.1.call-done = f32[1024,1024]{1,0:T(8,128)} async-done(((f32[2048,1024]{1,0:T(8,128)}), f32[1024,1024]{1,0:T(8,128)}) %reduce-scatter.17.cloned.1.call-update) | async-done | bytes 4194320 | tf_op jit(solution)/shard_map/reduce_scatter | solution.py:279
  1405.5 40.0 %all-reduce = (f32[1024]{0:T(1024)}, f32[1024]{0:T(1024)}, f32[1024]{0:T(1024)}, f32[1024]{0:T(1024)}, f32[1024]{0:T(1024)}, /*index=5*/f32[1024]{0:T(1024)}) all-reduce(f32[1024]{0:T(1024)S(1)} %get-tuple-element.227, f32[1024]{0:T(1024)S(1)} %get-tuple-element.232, ...), channel_id=1, replica_groups=mesh['dp'=16,'tensor'=2] {'dp','tensor'}, use_global_device_ids=true, to_apply=%region_25.26 | all-reduce | flops 6144 | bytes 49152 | tf_op jit(solution)/shard_map/psum | solution.py:313
  1445.5 5.2 fusion.91
  (320 shorter events, 180.7 us)
Async XLA Ops:
  7.2 7.1 copy-start.13
  7.2 43.7 %all-gather.13.cloned.1.call-start = ((), (), s32[]{:S(2)}) async-start(), calls=%async_computation.11 | async-start | bytes 1114112 | tf_op jit(solution)/shard_map/all_gather | solution.py:138
  7.9 100.7 %all-gather.11.cloned.1.call-start = ((), (), s32[]{:S(2)}) async-start(), calls=%async_computation.10 | async-start | bytes 6291456 | tf_op jit(solution)/shard_map/all_gather | solution.py:158
  8.7 5.0 copy-start.36
  11.3 7.1 copy-start.52
  11.3 7.3 copy-start.50
  11.3 7.3 copy-start.51
  16.4 132.4 %all-gather.15.cloned.1.call-start = ((), (), s32[]{:S(2)}) async-start(), calls=%async_computation.12 | async-start | bytes 1114112 | tf_op jit(solution)/shard_map/all_gather | solution.py:136
  17.2 170.6 %all-gather.17.cloned.1.call-start = ((), (), s32[]{:S(2)}) async-start(), calls=%async_computation.13 | async-start | bytes 1114112 | tf_op jit(solution)/shard_map/all_gather | solution.py:137
  17.7 252.7 %all-gather.19.cloned.1.call-start = ((), (), s32[]{:S(2)}) async-start(), calls=%async_computation.14 | async-start | bytes 1114112 | tf_op jit(solution)/shard_map/all_gather | solution.py:139
  18.3 358.0 %reduce-scatter.11.cloned.1.call-start = ((), (), s32[]{:S(2)}) async-start(), calls=%async_computation.15 | async-start | bytes 12582912 | tf_op jit(solution)/shard_map/reduce_scatter | solution.py:180
  263.9 6.5 copy-start.3
  263.9 6.5 copy-start.32
  278.0 98.4 %copy-start.14 = (bf16[1024,1024]{1,0:T(8,128)(2,1)S(1)}, bf16[1024,1024]{1,0:T(8,128)(2,1)}, u32[]{:S(2)}) copy-start(bf16[1024,1024]{1,0:T(8,128)(2,1)} %param.22) | copy-start | bytes 6291460
  278.0 151.3 %all-gather.23.cloned.1.call-start = ((), (), s32[]{:S(2)}) async-start(), calls=%async_computation.17 | async-start | bytes 4456448 | tf_op jit(solution)/shard_map/all_gather | solution.py:140
  278.7 208.0 %all-gather.21.cloned.1.call-start = ((), (), s32[]{:S(2)}) async-start(), calls=%async_computation.16 | async-start | bytes 6291456 | tf_op jit(solution)/shard_map/all_gather | solution.py:193
  383.3 161.9 %all-gather.27.cloned.1.call-start = ((), (), s32[]{:S(2)}) async-start(), calls=%async_computation.20 | async-start | bytes 6291456 | tf_op jit(solution)/shard_map/all_gather | solution.py:219
  384.0 214.0 %all-gather.25.cloned.1.call-start = ((), (), s32[]{:S(2)}) async-start(), calls=%async_computation.18 | async-start | bytes 4456448 | tf_op jit(solution)/shard_map/all_gather | solution.py:141
  384.6 352.9 %reduce-scatter.15.cloned.1.call-start = ((), (), s32[]{:S(2)}) async-start(), calls=%async_computation.21 | async-start | bytes 12582912 | tf_op jit(solution)/shard_map/reduce_scatter | solution.py:225
  598.0 29.9 %copy-start.56 = (bf16[1024,2048]{1,0:T(8,128)(2,1)S(1)}, bf16[1024,2048]{1,0:T(8,128)(2,1)}, u32[]{:S(2)}) copy-start(bf16[1024,2048]{1,0:T(8,128)(2,1)} %all-gather.23.cloned.1.call-done) | copy-start | bytes 12582916
  639.6 154.4 %reduce-scatter.13.cloned.1.call-start = ((), (), s32[]{:S(2)}) async-start(), calls=%async_computation.19 | async-start | bytes 6291456 | tf_op jit(solution)/shard_map/reduce_scatter | solution.py:199
  653.6 207.7 %all-gather.29.cloned.1.call-start = ((), (), s32[]{:S(2)}) async-start(), calls=%async_computation.22 | async-start | bytes 6291456 | tf_op jit(solution)/shard_map/all_gather | solution.py:242
  654.2 139.8 %copy-start.22 = (bf16[1024,1024]{1,0:T(8,128)(2,1)S(1)}, bf16[1024,1024]{1,0:T(8,128)(2,1)}, u32[]{:S(2)}) copy-start(bf16[1024,1024]{1,0:T(8,128)(2,1)} %param.39) | copy-start | bytes 6291460
  804.4 347.3 %reduce-scatter.27.cloned.1.call-start = ((), (), s32[]{:S(2)}) async-start(), calls=%async_computation.28 | async-start | bytes 4456448 | tf_op jit(solution)/shard_map/reduce_scatter | solution.py:305
  818.8 334.8 %reduce-scatter.29.cloned.1.call-start = ((), (), s32[]{:S(2)}) async-start(), calls=%async_computation.29 | async-start | bytes 4456448 | tf_op jit(solution)/shard_map/reduce_scatter | solution.py:308
  832.8 28.5 %copy-start.58 = (bf16[512,1024]{0,1:T(8,128)(2,1)S(1)}, bf16[512,1024]{0,1:T(8,128)(2,1)}, u32[]{:S(2)}) copy-start(bf16[512,1024]{0,1:T(8,128)(2,1)} %all-gather.19.cloned.1.call-done) | copy-start | bytes 3145732
  832.8 388.2 %reduce-scatter.25.cloned.1.call-start = ((), (), s32[]{:S(2)}) async-start(), calls=%async_computation.27 | async-start | bytes 1114112 | tf_op jit(solution)/shard_map/reduce_scatter | solution.py:302
  869.9 5.9 copy-start.27
  881.6 4.9 copy-start.4
  881.6 4.9 copy-start.33
  881.6 340.9 %reduce-scatter.19.cloned.1.call-start = ((), (), s32[]{:S(2)}) async-start(), calls=%async_computation.24 | async-start | bytes 1114112 | tf_op jit(solution)/shard_map/reduce_scatter | solution.py:293
  886.7 4.6 copy-start.11
  914.1 15.8 %copy-start.1 = (f32[8,512,1024]{2,1,0:T(8,128)S(1)}, f32[8,512,1024]{2,1,0:T(8,128)}, u32[]{:S(2)}) copy-start(f32[8,512,1024]{2,1,0:T(8,128)} %get-tuple-element.461) | copy-start | bytes 50331652 | tf_op jit(solution)/shard_map/while
  937.7 9.3 copy-start.6
  937.7 9.3 copy-start.9
  937.7 9.3 copy-start.16
  961.2 18.9 %copy-start = (f32[8,512,1024]{2,1,0:T(8,128)S(1)}, f32[8,512,1024]{2,1,0:T(8,128)}, u32[]{:S(2)}) copy-start(f32[8,512,1024]{2,1,0:T(8,128)} %get-tuple-element.465) | copy-start | bytes 50331652 | tf_op jit(solution)/shard_map/while
  961.2 19.5 %copy-start.5 = (f32[8,64,1024]{2,1,0:T(8,128)S(1)}, f32[8,64,1024]{2,1,0:T(8,128)}, u32[]{:S(2)}) copy-start(f32[8,64,1024]{2,1,0:T(8,128)} %fusion.205) | copy-start | bytes 6291460 | tf_op jit(solution)/shard_map/while
  984.4 11.6 slice-start
  990.8 5.2 slice-start.1
  990.8 5.4 copy-start.23
  1028.1 15.8 %copy-start.1 = (f32[8,512,1024]{2,1,0:T(8,128)S(1)}, f32[8,512,1024]{2,1,0:T(8,128)}, u32[]{:S(2)}) copy-start(f32[8,512,1024]{2,1,0:T(8,128)} %get-tuple-element.461) | copy-start | bytes 50331652 | tf_op jit(solution)/shard_map/while
  1051.7 9.3 copy-start.6
  1051.7 9.3 copy-start.9
  1051.7 9.3 copy-start.16
  1074.7 18.4 %copy-start = (f32[8,512,1024]{2,1,0:T(8,128)S(1)}, f32[8,512,1024]{2,1,0:T(8,128)}, u32[]{:S(2)}) copy-start(f32[8,512,1024]{2,1,0:T(8,128)} %get-tuple-element.465) | copy-start | bytes 50331652 | tf_op jit(solution)/shard_map/while
  1074.7 19.0 %copy-start.5 = (f32[8,64,1024]{2,1,0:T(8,128)S(1)}, f32[8,64,1024]{2,1,0:T(8,128)}, u32[]{:S(2)}) copy-start(f32[8,64,1024]{2,1,0:T(8,128)} %fusion.205) | copy-start | bytes 6291460 | tf_op jit(solution)/shard_map/while
  1097.4 11.3 slice-start
  1103.6 5.1 slice-start.1
  1103.6 5.3 copy-start.23
  1113.7 5.9 copy-start.53
  1123.0 118.1 %reduce-scatter.23.cloned.1.call-start = ((), (), s32[]{:S(2)}) async-start(), calls=%async_computation.26 | async-start | bytes 1114112 | tf_op jit(solution)/shard_map/reduce_scatter | solution.py:299
  1129.3 171.9 %reduce-scatter.21.cloned.1.call-start = ((), (), s32[]{:S(2)}) async-start(), calls=%async_computation.25 | async-start | bytes 1114112 | tf_op jit(solution)/shard_map/reduce_scatter | solution.py:296
  1129.5 5.9 copy-start.55
  1138.9 262.9 %reduce-scatter.17.cloned.1.call-start = ((), (), s32[]{:S(2)}) async-start(), calls=%async_computation.23 | async-start | bytes 12582912 | tf_op jit(solution)/shard_map/reduce_scatter | solution.py:279
  1151.6 7.9 copy-start.44
  1151.6 250.1 %copy-start.15 = (bf16[1024,1024]{1,0:T(8,128)(2,1)S(1)}, bf16[1024,1024]{1,0:T(8,128)(2,1)}, u32[]{:S(2)}) copy-start(bf16[1024,1024]{1,0:T(8,128)(2,1)} %param.22) | copy-start | bytes 6291460
  1151.6 250.1 %copy-start.35 = (f32[1024]{0:T(1024)S(1)}, f32[1024]{0:T(1024)}, u32[]{:S(2)}) copy-start(f32[1024]{0:T(1024)} %copy-done.34) | copy-start | bytes 12292
  1151.7 250.1 %copy-start.37 = (f32[1024]{0:T(1024)S(1)}, f32[1024]{0:T(1024)}, u32[]{:S(2)}) copy-start(f32[1024]{0:T(1024)} %copy-done.36) | copy-start | bytes 12292
  1151.7 250.1 %copy-start.39 = (f32[1024]{0:T(1024)S(1)}, f32[1024]{0:T(1024)}, u32[]{:S(2)}) copy-start(f32[1024]{0:T(1024)} %copy-done.38) | copy-start | bytes 12292
  1157.4 248.1 %copy-start.40 = (f32[1024]{0:T(1024)S(1)}, f32[1024]{0:T(1024)}, u32[]{:S(2)}) copy-start(f32[1024]{0:T(1024)} %get-tuple-element.225) | copy-start | bytes 12292
  1157.4 248.1 %copy-start.41 = (f32[1024]{0:T(1024)S(1)}, f32[1024]{0:T(1024)}, u32[]{:S(2)}) copy-start(f32[1024]{0:T(1024)} %get-tuple-element.231) | copy-start | bytes 12292
  1157.4 248.1 %copy-start.42 = (f32[1024]{0:T(1024)S(1)}, f32[1024]{0:T(1024)}, u32[]{:S(2)}) copy-start(f32[1024]{0:T(1024)} %get-tuple-element.282) | copy-start | bytes 12292
  1157.4 248.1 %copy-start.43 = (f32[1024]{0:T(1024)S(1)}, f32[1024]{0:T(1024)}, u32[]{:S(2)}) copy-start(f32[1024]{0:T(1024)} %get-tuple-element.308) | copy-start | bytes 12292
  (38 other events, 94.6 us)
Sparse Core Ops, SparseCore 0:
  10.2 40.6 all-gather.12
  53.0 55.6 all-gather.10
  110.8 37.9 all-gather.14
  150.8 36.8 all-gather.16
  189.7 36.8 all-gather.18
  278.1 98.1 reduce-scatter.10
  378.7 50.5 all-gather.22
  431.5 55.2 all-gather.20
  488.4 56.7 all-gather.26
  547.4 50.5 all-gather.24
  639.7 97.7 reduce-scatter.14
  739.6 54.3 reduce-scatter.12
  804.5 56.7 all-gather.28
  865.5 72.4 reduce-scatter.26
  941.7 71.4 reduce-scatter.28
  1017.1 56.4 reduce-scatter.24
  1123.1 57.5 reduce-scatter.18
  1184.7 56.3 reduce-scatter.22
  1244.7 56.4 reduce-scatter.20
  1303.5 98.2 reduce-scatter.16
where the time goes:
time: 1470 us; the launch traced here: 1460 us
  waiting for transfers between devices  779 us (53%)
  matrix products  329 us (22%)
  other arithmetic  132 us (9%)
  blocking collectives  101 us (7%)
  local copies, waits for them, and re-layouts  98.3 us (7%)
  between operations  15.1 us (1%)
    reduce_scatter x1, waiting for transfers between devices, shards(): lax.psum_scatter(jnp.einsum('tc,dc->td', part_query, query_w, preferred_e...  99 us
    reduce_scatter x1, waiting for transfers between devices, shards(): lax.psum_scatter(jnp.dot(lax.slice_in_dim(context, 0, own_rows * lax.axis...  97.5 us
    reduce_scatter x1, waiting for transfers between devices, shards(): lax.psum_scatter(jnp.einsum('tf,df->td', lax.slice_in_dim(up_grad, 0, own...  83.2 us
    dot_general x8, matrix products, block_scores(): jnp.einsum('qhd,khd->hqk', query_rows, keys_all, preferred_element_type=j...  76.7 us
    psum x1, blocking collectives, shards(): lax.psum((query_b_grad, value_b_grad, up_b_grad), 'dp')  61.5 us
    reduce_scatter x1, waiting for transfers between devices, shards(): lax.psum_scatter(key_w_grad.astype(jnp.bfloat16), 'dp', scatter_dimension...  58.6 us
    all_gather x1, waiting for transfers between devices, shards(): lax.all_gather(out_one.astype(jnp.bfloat16), 'tensor', axis=0, tiled=True)  57.8 us
    all_gather x1, waiting for transfers between devices, shards(): lax.all_gather(out_two.astype(jnp.bfloat16), 'tensor', axis=0, tiled=True)  57.5 us
  transfers between devices with their start and end apart: 20, of which 15 were waited for; matrix products, arithmetic and copies ran while one was open for 32% of the time, Pallas kernels for 0%

commit v1 on v0

v1 whole, which is shorter than its diff:
```python
import jax
import jax.numpy as jnp
from jax import lax
from jax.experimental import pallas as pl
from jax.experimental.pallas import tpu as pltpu
from jax.sharding import PartitionSpec as P

HEADS = 16
HDIM = 64
SEQ_LEN = 1024
SPAN = 256
LANES = 128
FAR = -1e30

epsilon = 1e-05
f32 = jnp.float32
bf16 = jnp.bfloat16


def normalize(field, norm_gain, norm_shift):
    average = jnp.mean(field, -1, keepdims=True)
    centred = field - average
    factor = lax.rsqrt(jnp.mean(centred * centred, -1, keepdims=True) + epsilon)
    normed = centred * factor
    return (normed * norm_gain + norm_shift, normed, factor)


def norm_back(upstream, normed, factor, norm_gain):
    scaled = upstream * norm_gain
    return factor * (
        scaled
        - jnp.mean(scaled, -1, keepdims=True)
        - normed * jnp.mean(scaled * normed, -1, keepdims=True)
    )


def gelu_tanh(field):
    return jax.nn.gelu(field, approximate=True)


def dot(a, b):
    return jnp.dot(a, b, preferred_element_type=f32)


def dot_nt(a, b):
    return lax.dot_general(a, b, (((1,), (1,)), ((), ())), preferred_element_type=f32)


def dot_tn(a, b):
    return lax.dot_general(a, b, (((0,), (0,)), ((), ())), preferred_element_type=f32)


def split_three(field):
    one = field.astype(bf16)
    rest = field - one.astype(f32)
    two = rest.astype(bf16)
    three = (rest - two.astype(f32)).astype(bf16)
    return one.astype(f32), two.astype(f32), three.astype(f32)


def place_columns(doc_lengths, slopes):
    seq_count, docs = doc_lengths.shape
    doc_ends = jnp.cumsum(doc_lengths, axis=1)
    places = jnp.arange(SEQ_LEN, dtype=jnp.int32)
    segment_ids = jnp.sum((places[None, :, None] >= doc_ends[:, None, :]).astype(jnp.int32), axis=2)
    low = (places % 128).astype(f32)
    high = (places - places % 128).astype(f32)
    pairs = jnp.broadcast_to(
        jnp.stack([high, low, high, low], -1)[None], (seq_count, SEQ_LEN, 4)
    )
    none = jnp.zeros((seq_count, SEQ_LEN, 4), f32)
    same = (segment_ids[:, :, None] == jnp.arange(docs)[None, None, :]).astype(f32)
    ones = jnp.ones((seq_count, SEQ_LEN, 3), f32)
    rest = jnp.zeros((seq_count, SEQ_LEN, HDIM - 11 - docs), f32)
    query_half = jnp.concatenate([none, pairs, 0.0 * ones, FAR * (1.0 - same), rest], -1)
    key_half = jnp.concatenate([pairs, none, ones, same, rest], -1)
    query_base = jnp.concatenate([query_half, query_half], -1).astype(bf16)
    key_base = jnp.concatenate([key_half, key_half], -1).astype(bf16)
    first = slopes.astype(bf16).astype(f32)
    second = (slopes - first).astype(bf16).astype(f32)
    four = jnp.stack([first, first, second, second], -1)
    heads = slopes.shape[0]
    blank = jnp.zeros((heads, 4), f32)
    tail = jnp.zeros((heads, HDIM - 8), f32)
    query_line = jnp.concatenate([four, blank, tail], -1)
    key_line = jnp.concatenate([blank, -four, tail], -1)
    lines = jnp.stack([query_line, key_line], 1)
    lines = jnp.concatenate([lines, lines], -1)
    lines = jnp.concatenate([lines, jnp.zeros((heads, 6, LANES), f32)], 1)
    return query_base, key_base, lines.astype(bf16)


def lane_of(rows):
    return lax.broadcasted_iota(jnp.int32, (rows, LANES), 1)


def forward_kernel(qkv_ref, qbase_ref, kbase_ref, lines_ref, out_ref, total_ref):
    upper = lane_of(SEQ_LEN) >= HDIM
    upper_rows = lane_of(SPAN) >= HDIM
    query = (qkv_ref[:, :LANES].astype(f32) * (HDIM**-0.5)).astype(bf16)
    keys = qkv_ref[:, LANES : 2 * LANES]
    values = qkv_ref[:, 2 * LANES :]
    keep = lax.broadcasted_iota(jnp.int32, (SPAN, SPAN), 1) <= lax.broadcasted_iota(
        jnp.int32, (SPAN, SPAN), 0
    )
    found = []
    for head in range(2):
        mine = upper if head else jnp.logical_not(upper)
        query_full = jnp.where(mine, query, qbase_ref[0] + lines_ref[head, 0:1, :])
        keys_full = jnp.where(mine, keys, kbase_ref[0] + lines_ref[head, 1:2, :])
        per_head = []
        for start in range(0, SEQ_LEN, SPAN):
            rows = query_full[start : start + SPAN]
            near = jnp.where(keep, dot_nt(rows, keys_full[start : start + SPAN]), FAR)
            row_max = jnp.max(near, -1, keepdims=True)
            if start:
                past = dot_nt(rows, keys_full[:start])
                row_max = jnp.maximum(row_max, jnp.max(past, -1, keepdims=True))
            near = jnp.exp(near - row_max)
            row_sum = jnp.sum(near, -1, keepdims=True)
            mixed = dot(near.astype(bf16), values[start : start + SPAN])
            if start:
                past = jnp.exp(past - row_max)
                row_sum = row_sum + jnp.sum(past, -1, keepdims=True)
                mixed = mixed + dot(past.astype(bf16), values[:start])
            per_head.append((mixed / row_sum, row_max + jnp.log(row_sum)))
        found.append(per_head)
    for index, start in enumerate(range(0, SEQ_LEN, SPAN)):
        lower_out, lower_total = found[0][index]
        upper_out, upper_total = found[1][index]
        out_ref[start : start + SPAN, :] = jnp.where(upper_rows, upper_out, lower_out).astype(bf16)
        total_ref[start : start + SPAN, :] = jnp.where(upper_rows, upper_total, lower_total)


def backward_kernel(
    qkv_ref, qbase_ref, kbase_ref, lines_ref, out_ref, total_ref, grad_ref, back_ref, hold_ref
):
    lane = lane_of(SEQ_LEN)
    upper = lane >= HDIM
    column = lane % HDIM
    upper_rows = lane_of(SPAN) >= HDIM
    query = (qkv_ref[:, :LANES].astype(f32) * (HDIM**-0.5)).astype(bf16)
    keys = qkv_ref[:, LANES : 2 * LANES]
    values = qkv_ref[:, 2 * LANES :]
    grads = grad_ref[...]
    keep = lax.broadcasted_iota(jnp.int32, (SPAN, SPAN), 0) <= lax.broadcasted_iota(
        jnp.int32, (SPAN, SPAN), 1
    )
    meets = grads.astype(f32) * out_ref[...].astype(f32)
    three_ones = jnp.where(column < 3, 1.0, 0.0).astype(bf16)
    for head in range(2):
        mine = upper if head else jnp.logical_not(upper)
        total = total_ref[:, HDIM : HDIM + 1] if head else total_ref[:, 0:1]
        one, two, three = split_three(-total)
        extra = jnp.where(
            column == 8, one, jnp.where(column == 9, two, jnp.where(column == 10, three, 0.0))
        ).astype(bf16)
        query_full = jnp.where(mine, query, qbase_ref[0] + lines_ref[head, 0:1, :] + extra)
        keys_full = jnp.where(mine, keys, kbase_ref[0] + lines_ref[head, 1:2, :])
        delta = jnp.sum(jnp.where(mine, meets, 0.0), -1, keepdims=True)
        one, two, three = split_three(-delta)
        extra = jnp.where(
            column == 0, one, jnp.where(column == 1, two, jnp.where(column == 2, three, 0.0))
        ).astype(bf16)
        grads_full = jnp.where(mine, grads, extra)
        values_full = jnp.where(mine, values, three_ones)
        for start in range(0, SEQ_LEN, SPAN):
            here = slice(start, start + SPAN)
            later = slice(start + SPAN, SEQ_LEN)
            near = jnp.where(keep, dot_nt(keys_full[here], query_full[here]), FAR)
            near = jnp.exp(near)
            near_grad = (near * dot_nt(values_full[here], grads_full[here])).astype(bf16)
            value_grad = dot(near.astype(bf16), grads[here])
            key_grad = dot(near_grad, query[here])
            query_near = dot_tn(near_grad, keys[here])
            if start:
                hold_ref[here, :] += query_near
            else:
                hold_ref[here, :] = query_near
            if start + SPAN < SEQ_LEN:
                past = jnp.exp(dot_nt(keys_full[here], query_full[later]))
                past_grad = (past * dot_nt(values_full[here], grads_full[later])).astype(bf16)
                value_grad = value_grad + dot(past.astype(bf16), grads[later])
                key_grad = key_grad + dot(past_grad, query[later])
                query_past = dot_tn(past_grad, keys[here])
                if start:
                    hold_ref[later, :] += query_past
                else:
                    hold_ref[later, :] = query_past
            key_grad = key_grad.astype(bf16)
            value_grad = value_grad.astype(bf16)
            if head:
                key_grad = jnp.where(upper_rows, key_grad, back_ref[here, LANES : 2 * LANES])
                value_grad = jnp.where(upper_rows, value_grad, back_ref[here, 2 * LANES :])
            back_ref[here, LANES : 2 * LANES] = key_grad
            back_ref[here, 2 * LANES :] = value_grad
        query_grad = (hold_ref[...] * (HDIM**-0.5)).astype(bf16)
        if head:
            query_grad = jnp.where(upper, query_grad, back_ref[:, :LANES])
        back_ref[:, :LANES] = query_grad


def attention_specs():
    return [
        pl.BlockSpec((SEQ_LEN, 3 * LANES), lambda s, h: (s, h)),
        pl.BlockSpec((1, SEQ_LEN, LANES), lambda s, h: (s, 0, 0)),
        pl.BlockSpec((1, SEQ_LEN, LANES), lambda s, h: (s, 0, 0)),
        pl.BlockSpec((2, 8, LANES), lambda s, h: (h, 0, 0)),
    ]


def pair_spec():
    return pl.BlockSpec((SEQ_LEN, LANES), lambda s, h: (s, h))


def attend_forward(qkv, columns):
    rows, width = qkv.shape
    pairs = width // (3 * LANES)
    seqs = rows // SEQ_LEN
    work = seqs * pairs * 2 * SEQ_LEN * SEQ_LEN
    return pl.pallas_call(
        forward_kernel,
        grid=(seqs, pairs),
        in_specs=attention_specs(),
        out_specs=[pair_spec(), pair_spec()],
        out_shape=[
            jax.ShapeDtypeStruct((rows, pairs * LANES), bf16),
            jax.ShapeDtypeStruct((rows, pairs * LANES), f32),
        ],
        compiler_params=pltpu.CompilerParams(vmem_limit_bytes=40 * 1024 * 1024),
        cost_estimate=pl.CostEstimate(
            flops=work * 320, bytes_accessed=rows * width * 4, transcendentals=work * 5 // 8
        ),
    )(qkv, *columns)


def attend_backward(qkv, columns, context, totals, grads):
    rows, width = qkv.shape
    pairs = width // (3 * LANES)
    seqs = rows // SEQ_LEN
    work = seqs * pairs * 2 * SEQ_LEN * SEQ_LEN
    return pl.pallas_call(
        backward_kernel,
        grid=(seqs, pairs),
        in_specs=attention_specs() + [pair_spec(), pair_spec(), pair_spec()],
        out_specs=pl.BlockSpec((SEQ_LEN, 3 * LANES), lambda s, h: (s, h)),
        out_shape=jax.ShapeDtypeStruct((rows, width), bf16),
        scratch_shapes=[pltpu.VMEM((SEQ_LEN, LANES), f32)],
        compiler_params=pltpu.CompilerParams(vmem_limit_bytes=40 * 1024 * 1024),
        cost_estimate=pl.CostEstimate(
            flops=work * 800, bytes_accessed=rows * width * 8, transcendentals=work * 5 // 8
        ),
    )(qkv, *columns, context, totals, grads)


def interleave(query, key, value):
    rows, width = query.shape
    parts = [part.reshape(rows, width // LANES, LANES) for part in (query, key, value)]
    return jnp.stack(parts, 2).reshape(rows, 3 * width)


def separate(joined):
    rows, width = joined.shape
    parts = joined.reshape(rows, width // (3 * LANES), 3, LANES)
    return [parts[:, :, which].reshape(rows, width // 3) for which in range(3)]


def shards(
    tokens,
    doc_lengths,
    ln1_gain,
    ln1_bias,
    w_query,
    b_query,
    w_key,
    w_value,
    b_value,
    w_dense,
    b_dense,
    ln2_gain,
    ln2_bias,
    w_up,
    b_up,
    w_down,
    b_down,
    out_grad,
):
    own_rows = tokens.shape[0]
    groups = lax.axis_size("tensor")
    group = lax.axis_index("tensor")
    alone = own_rows % SEQ_LEN == 0
    parts = groups if alone else 1
    axes = ("tensor", "dp") if alone else "dp"
    if alone:
        seqs = own_rows // SEQ_LEN
        doc_lengths = lax.dynamic_slice_in_dim(doc_lengths, group * seqs, seqs)

    def gathered(shard):
        full = lax.all_gather(shard, axes, axis=0, tiled=True)
        full = full.reshape((parts, full.shape[0] // parts, full.shape[1]))
        return [full[part] for part in range(parts)]

    def scattered(pieces):
        stacked = jnp.concatenate([piece.astype(bf16) for piece in pieces], 0)
        return lax.psum_scatter(stacked, axes, scatter_dimension=0, tiled=True).astype(f32)

    def spread(rows):
        return rows if alone else lax.all_gather(rows, "tensor", axis=0, tiled=True)

    def collect(rows):
        if alone:
            return rows
        return lax.psum_scatter(
            rows.astype(bf16), "tensor", scatter_dimension=0, tiled=True
        ).astype(f32)

    def total_of(pieces):
        result = pieces[0]
        for piece in pieces[1:]:
            result = result + piece
        return result

    width = w_query.shape[1]
    local_heads = width // HDIM
    qkv_bias = interleave(b_query[None], jnp.zeros_like(b_query)[None], b_value[None])
    biases = jnp.concatenate([qkv_bias, b_up[None]], -1)
    if alone:
        biases = lax.all_gather(biases, "tensor", axis=0, tiled=True)
    biases = biases.astype(f32)

    qkv_w = gathered(interleave(w_query, w_key, w_value))
    dense_w = gathered(w_dense.T)
    up_w = gathered(w_up)
    down_w = gathered(w_down.T)

    columns = []
    for part in range(parts):
        first_head = (part if alone else group) * local_heads
        head_number = first_head + jnp.arange(local_heads, dtype=jnp.int32) + 1
        slopes = 2.0 ** (-8.0 * head_number.astype(f32) / HEADS)
        columns.append(place_columns(doc_lengths, slopes))

    field = tokens.astype(f32)
    gain_one = ln1_gain.astype(f32)
    gain_two = ln2_gain.astype(f32)
    out_one, normed_one, factor_one = normalize(field, gain_one, ln1_bias.astype(f32))
    norm_rows = spread(out_one.astype(bf16))
    grad_rows = spread(out_grad)
    every = range(parts)
    qkv = [
        (dot(norm_rows, qkv_w[part]) + biases[part, : 3 * width]).astype(bf16) for part in every
    ]
    context, totals = zip(*[attend_forward(qkv[part], columns[part]) for part in every])
    hidden_one = (
        field
        + collect(total_of([dot_nt(context[part], dense_w[part]) for part in every]))
        + b_dense.astype(f32)
    )
    out_two, normed_two, factor_two = normalize(hidden_one, gain_two, ln2_bias.astype(f32))
    mlp_rows = spread(out_two.astype(bf16))
    activated, slope_rows = [], []
    for part in every:
        up_field = dot(mlp_rows, up_w[part]) + biases[part, 3 * width :]
        gelu_field, gelu_pull = jax.vjp(gelu_tanh, up_field)
        activated.append(gelu_field.astype(bf16))
        slope_rows.append(gelu_pull(jnp.ones_like(up_field))[0].astype(bf16))
    branch_sum = collect(total_of([dot_nt(activated[part], down_w[part]) for part in every]))
    mixed = (hidden_one + branch_sum + b_down.astype(f32)).astype(bf16)

    up_grad = [
        (dot(grad_rows, down_w[part]) * slope_rows[part].astype(f32)).astype(bf16)
        for part in every
    ]
    down_w_sum = scattered([dot_tn(grad_rows, activated[part]) for part in every]).T
    up_w_sum = scattered([dot_tn(mlp_rows, up_grad[part]) for part in every])
    norm_two_grad = collect(total_of([dot_nt(up_grad[part], up_w[part]) for part in every]))
    outer_grad = out_grad.astype(f32)
    hidden_grad = outer_grad + norm_back(norm_two_grad, normed_two, factor_two, gain_two)
    branch_rows = spread(hidden_grad.astype(bf16))
    context_grad = [dot(branch_rows, dense_w[part]).astype(bf16) for part in every]
    dense_w_sum = scattered([dot_tn(branch_rows, context[part]) for part in every]).T
    qkv_grad = [
        attend_backward(qkv[part], columns[part], context[part], totals[part], context_grad[part])
        for part in every
    ]
    qkv_w_sum = scattered([dot_tn(norm_rows, qkv_grad[part]) for part in every])
    query_w_sum, key_w_sum, value_w_sum = separate(qkv_w_sum)
    norm_one_grad = collect(total_of([dot_nt(qkv_grad[part], qkv_w[part]) for part in every]))
    tokens_grad = (hidden_grad + norm_back(norm_one_grad, normed_one, factor_one, gain_one)).astype(
        bf16
    )
    bias_axes = ("dp", "tensor") if alone else "dp"
    up_b_sum = lax.psum(
        jnp.concatenate([jnp.sum(piece.astype(f32), 0) for piece in up_grad]), bias_axes
    )
    qkv_b_sum = lax.psum(
        jnp.concatenate([jnp.sum(piece.astype(f32), 0) for piece in qkv_grad]), bias_axes
    )
    if alone:
        up_b_sum = lax.dynamic_slice_in_dim(up_b_sum, group * b_up.shape[0], b_up.shape[0])
        qkv_b_sum = lax.dynamic_slice_in_dim(qkv_b_sum, group * 3 * width, 3 * width)
    query_b_sum, _, value_b_sum = [piece[0] for piece in separate(qkv_b_sum[None])]
    early = (
        jnp.sum(hidden_grad, 0),
        jnp.sum(norm_two_grad * normed_two, 0),
        jnp.sum(norm_two_grad, 0),
        jnp.sum(outer_grad, 0),
    )
    late = (jnp.sum(norm_one_grad * normed_one, 0), jnp.sum(norm_one_grad, 0))
    dense_b_sum, gain_two_sum, shift_two_sum, down_b_sum = lax.psum(early, ("dp", "tensor"))
    gain_one_sum, shift_one_sum = lax.psum(late, ("dp", "tensor"))
    return (
        mixed,
        tokens_grad,
        gain_one_sum,
        shift_one_sum,
        query_w_sum,
        query_b_sum,
        key_w_sum,
        value_w_sum,
        value_b_sum,
        dense_w_sum,
        dense_b_sum,
        gain_two_sum,
        shift_two_sum,
        up_w_sum,
        up_b_sum,
        down_w_sum,
        down_b_sum,
    )


def solution(mesh):
    placed = (
        P(("dp", "tensor"), None),
        P("dp", None),
        P(),
        P(),
        P("dp", "tensor"),
        P("tensor"),
        P("dp", "tensor"),
        P("dp", "tensor"),
        P("tensor"),
        P("tensor", "dp"),
        P(),
        P(),
        P(),
        P("dp", "tensor"),
        P("tensor"),
        P("tensor", "dp"),
        P(),
        P(("dp", "tensor"), None),
    )
    return jax.shard_map(
        shards,
        mesh=mesh,
        in_specs=placed,
        out_specs=(
            P(("dp", "tensor"), None),
            P(("dp", "tensor"), None),
            P(),
            P(),
            P("dp", "tensor"),
            P("tensor"),
            P("dp", "tensor"),
            P("dp", "tensor"),
            P("tensor"),
            P("tensor", "dp"),
            P(),
            P(),
            P(),
            P("dp", "tensor"),
            P("tensor"),
            P("tensor", "dp"),
            P(),
        ),
        check_vma=False,
    )
```

time: 1470 us -> 925 us (0.63)
  waiting for transfers between devices: 779 us -> 522 us
  matrix products: 329 us -> 160 us
  other arithmetic: 132 us -> 45.8 us
  Pallas kernels: 0 us -> 76.9 us
  blocking collectives: 101 us -> 46.5 us
  local copies, waits for them, and re-layouts: 98.3 us -> 48.1 us
    all_gather x10 -> x4, waiting for transfers between devices: 367 us -> 187 us  [gathered(): full = lax.all_gather(shard, axes, axis=0, tiled=True)]
    dot_general x46 -> x24, matrix products: 329 us -> 160 us  [the longest x8 57.9 us: dot(): return jnp.dot(a, b, preferred_element_type=f32)]
    pallas_call x0 -> x4, Pallas kernels: none -> 76.9 us  [the longest x2 48.3 us: attend_backward(): pl.pallas_call(backward_kernel, grid=(seqs, pairs), in_specs=attention_sp...]
    reduce_scatter x10 -> x4, waiting for transfers between devices: 407 us -> 334 us  [scattered(): lax.psum_scatter(stacked, axes, scatter_dimension=0, tiled=True).astype(f32)]
    convert_element_type x30 -> x12, other arithmetic: 78.4 us -> 7.53 us  [the longest x1 1.99 us: shards(): mlp_rows = spread(out_two.astype(bf16))]
    psum x2 -> x1, blocking collectives: 101 us -> 41.2 us  [shards(): gain_one_sum, shift_one_sum = lax.psum(late, ('dp', 'tensor'))]
    while x84 -> x0, local copies, waits for them, and re-layouts: 38.9 us -> none
    reduce_sum x10 -> x4, other arithmetic: 33.6 us -> 6.46 us  [the longest x1 3.32 us: shards(): jnp.sum(hidden_grad, 0)]
  transfers between devices with their start and end apart: 20 -> 8, of which waited for: 15 -> 7; matrix products, arithmetic and copies ran while one was open for 32% -> 20% of each run, Pallas kernels for 0% -> 8%
where the time goes in v1:
time: 925 us; the launch traced here: 915 us
  waiting for transfers between devices  522 us (56%)
  matrix products  160 us (17%)
  Pallas kernels  76.9 us (8%)
  local copies, waits for them, and re-layouts  48.1 us (5%)
  blocking collectives  46.5 us (5%)
  other arithmetic  45.8 us (5%)
  between operations  15.1 us (2%)
    reduce_scatter x4, waiting for transfers between devices, scattered(): lax.psum_scatter(stacked, axes, scatter_dimension=0, tiled=True).astype(f32)  334 us
    all_gather x4, waiting for transfers between devices, gathered(): full = lax.all_gather(shard, axes, axis=0, tiled=True)  187 us
    dot_general x8, matrix products, dot(): return jnp.dot(a, b, preferred_element_type=f32)  57.9 us
    dot_general x8, matrix products, dot_nt(): lax.dot_general(a, b, (((1,), (1,)), ((), ())), preferred_element_type=f32)  56.6 us
    pallas_call x2, Pallas kernels, attend_backward(): pl.pallas_call(backward_kernel, grid=(seqs, pairs), in_specs=attention_sp...  48.3 us
    dot_general x8, matrix products, dot_tn(): lax.dot_general(a, b, (((0,), (0,)), ((), ())), preferred_element_type=f32)  45.9 us
    psum x1, blocking collectives, shards(): gain_one_sum, shift_one_sum = lax.psum(late, ('dp', 'tensor'))  41.2 us
    unnamed x101, local copies, waits for them, and re-layouts  29.5 us
  transfers between devices with their start and end apart: 8, of which 7 were waited for; matrix products, arithmetic and copies ran while one was open for 20% of the time, Pallas kernels for 8%

profile of v1, /device:TPU:0, one launch (start us, length us, event | category | flops | bytes accessed | tf_op | source)
XLA Modules:
  0.0 915.3 jit_solution(3227459488651997477)
XLA Ops:
  8.1 0.9 stack_reshape.17
  19.0 5.3 all-gather
  24.6 2.9 copy.101
  27.4 4.6 copy.112
  33.3 4.4 concatenate.103.qbase_ref
  37.7 0.9 fusion.66
  39.4 4.3 concatenate.106.kbase_ref
  44.9 38.8 %all-gather.6.cloned.1.call-done = bf16[2048,1536]{1,0:T(8,128)(2,1)} async-done(((bf16[64,1536]{1,0:T(8,128)(2,1)}), bf16[2048,1536]{1,0:T(8,128)(2,1)}) %all-gather.6.cloned.1.call-update) | async-done | bytes 6291472 | tf_op jit(solution)/shard_map/all_gather | solution.py:299
  83.8 5.8 add_convert_fusion.1.qkv_ref
  89.6 14.3 %shard_map.305 = (bf16[1024,512]{1,0:T(8,128)(2,1)S(1)}, f32[1024,512]{1,0:T(8,128)S(1)}) custom-call(bf16[1024,1536]{1,0:T(8,128)(2,1)S(1)} %add_convert_fusion.1.qkv_ref, bf16[1,1024,128]{2,1,0:T(8,128)(2,1)S(1)} %concatenate.103.qbase_ref, bf16[1,1024,128]{2,1,0:T(8,128)(2,1)S(1)} %concatenate.106.kbase_ref, ...), custom_call_target="tpu_custom_call" | custom-call | flops 2684354560 | bytes 6291456 | tf_op jit(solution)/shard_map/pallas_call | solution.py:221
  103.9 1.3 copy-done.10
  105.2 4.0 add_convert_fusion.qkv_ref
  109.2 14.3 %shard_map.306 = (bf16[1024,512]{1,0:T(8,128)(2,1)S(1)}, f32[1024,512]{1,0:T(8,128)S(1)}) custom-call(bf16[1024,1536]{1,0:T(8,128)(2,1)S(1)} %add_convert_fusion.qkv_ref, bf16[1,1024,128]{2,1,0:T(8,128)(2,1)S(1)} %concatenate.103.qbase_ref, bf16[1,1024,128]{2,1,0:T(8,128)(2,1)S(1)} %concatenate.106.kbase_ref, bf16[8,8,128]{2,1,0:T(8,128)(2,1)S(1)} %fusion.69.lines_ref), custom_call_target="tpu_custom_call" | custom-call | flops 2684354560 | bytes 6291456 | tf_op jit(solution)/shard_map/pallas_call | solution.py:221
  123.5 1.7 copy-done.8
  125.2 1.3 copy-done.12
  126.5 15.1 %all-gather.8.cloned.1.call-done = bf16[2048,512]{1,0:T(8,128)(2,1)} async-done(((bf16[64,512]{1,0:T(8,128)(2,1)}), bf16[2048,512]{1,0:T(8,128)(2,1)}) %all-gather.8.cloned.1.call-update) | async-done | bytes 2097168 | tf_op jit(solution)/shard_map/all_gather | solution.py:299
  141.6 2.7 fusion.61
  144.3 1.5 fusion.86
  146.3 1.4 copy-done.14
  147.8 2.0 add_convert_fusion.3
  149.7 71.2 %all-gather.10.cloned.1.call-done = bf16[2048,2048]{1,0:T(8,128)(2,1)} async-done(((bf16[64,2048]{1,0:T(8,128)(2,1)}), bf16[2048,2048]{1,0:T(8,128)(2,1)}) %all-gather.10.cloned.1.call-update) | async-done | bytes 8388624 | tf_op jit(solution)/shard_map/all_gather | solution.py:299
  220.9 10.8 %fusion.35 = f32[1024,2048]{1,0:T(8,128)} fusion(bf16[1024,1024]{0,1:T(8,128)(2,1)} %add_convert_fusion.3, bf16[2048,2048]{1,0:T(8,128)(2,1)} %all-gather.10.cloned.1.call-done), kind=kOutput, calls=%fused_computation.69 | convolution fusion | flops 4294967296 | bytes 14680064 | tf_op jit(solution)/shard_map/dot_general | solution.py:42
  231.7 6.7 fusion.42
  238.4 61.4 %all-gather.12.cloned.1.call-done = bf16[2048,2048]{1,0:T(8,128)(2,1)} async-done(((bf16[64,2048]{1,0:T(8,128)(2,1)}), bf16[2048,2048]{1,0:T(8,128)(2,1)}) %all-gather.12.cloned.1.call-update) | async-done | bytes 8388624 | tf_op jit(solution)/shard_map/all_gather | solution.py:299
  299.8 13.5 %convert_reduce_fusion = (f32[2048]{0:T(1024)}, bf16[1024,2048]{1,0:T(8,128)(2,1)S(1)}) fusion(f32[1024,2048]{1,0:T(8,128)} %fusion.35, f32[2048]{0:T(1024)S(1)} %bitcast.92, bf16[1024,1024]{1,0:T(8,128)(2,1)} %param.35, bf16[2048,2048]{1,0:T(8,128)(2,1)} %all-gather.12.cloned.1.call-done), kind=kOutput, calls=%fused_computation.20 | convolution fusion | flops 4345296896 | bytes 18890752 | tf_op jit(solution)/shard_map/dot_general | solution.py:42
  313.4 9.8 %fusion.33 = f32[1024,1024]{0,1:T(8,128)} fusion(bf16[1024,2048]{1,0:T(8,128)(2,1)S(1)} %get-tuple-element.143, bf16[2048,2048]{1,0:T(8,128)(2,1)} %all-gather.10.cloned.1.call-done), kind=kOutput, calls=%fused_computation.67 | convolution fusion | flops 4294967296 | bytes 12582912 | tf_op jit(solution)/shard_map/dot_general | solution.py:46
  323.2 12.6 %convert_reduce_fusion.1 = (f32[2048]{0:T(1024)}, bf16[1024,2048]{1,0:T(8,128)(2,1)S(1)}) fusion(f32[1024,2048]{1,0:T(8,128)} %fusion.42, f32[2048]{0:T(1024)S(1)} %bitcast.89, bf16[1024,1024]{1,0:T(8,128)(2,1)S(1)} %copy-done.29, bf16[2048,2048]{1,0:T(8,128)(2,1)S(1)} %copy-done.40), kind=kOutput, calls=%fused_computation.21 | convolution fusion | flops 4345296896 | bytes 18890752 | tf_op jit(solution)/shard_map/dot_general | solution.py:42
  335.8 11.0 %multiply_reduce_fusion = (f32[1024]{0:T(1024)}, f32[1024]{0:T(1024)S(1)}, f32[1024]{0:T(1024)S(1)}, f32[1024]{0:T(1024)}, f32[1024,1024]{0,1:T(8,128)S(1)}) fusion(f32[1024,1024]{0,1:T(8,128)S(1)} %copy-done.15, f32[1024]{0:T(1024)S(1)} %add_rsqrt_fusion, f32[1024]{0:T(1024)S(1)} %broadcast_multiply_fusion.4, f32[1024]{0:T(1024)S(1)} %convert_element_type.453, ...), kind=kOutput, calls=%fused_computation.54 | convolution fusion | flops 4305448960 | bytes 21000192 | tf_op jit(solution)/shard_map/dot_general | solution.py:46
  346.8 3.3 fusion.83
  350.4 1.2 convolution_convert_fusion.4
  352.7 1.2 convolution_convert_fusion.5
  353.9 1.5 pad_maximum_fusion.3
  355.5 3.3 convolution_convert_fusion.6.grad_ref
  358.8 1.3 convolution_convert_fusion.7.grad_ref
  361.4 24.2 %shard_map.308 = bf16[1024,1536]{1,0:T(8,128)(2,1)S(1)} custom-call(bf16[1024,1536]{1,0:T(8,128)(2,1)S(1)} %copy-done.9, bf16[1,1024,128]{2,1,0:T(8,128)(2,1)S(1)} %concatenate.103.qbase_ref, bf16[1,1024,128]{2,1,0:T(8,128)(2,1)S(1)} %concatenate.106.kbase_ref, bf16[8,8,128]{2,1,0:T(8,128)(2,1)S(1)} %fusion.69.lines_ref, ...), custom_call_target="tpu_custom_call" | custom-call | flops 6710886400 | bytes 12582912 | tf_op jit(solution)/shard_map/pallas_call | solution.py:242
  385.7 24.1 %shard_map.307 = bf16[1024,1536]{1,0:T(8,128)(2,1)S(1)} custom-call(bf16[1024,1536]{1,0:T(8,128)(2,1)S(1)} %copy-done.7, bf16[1,1024,128]{2,1,0:T(8,128)(2,1)S(1)} %concatenate.103.qbase_ref, bf16[1,1024,128]{2,1,0:T(8,128)(2,1)S(1)} %concatenate.106.kbase_ref, bf16[8,8,128]{2,1,0:T(8,128)(2,1)S(1)} %concatenate.110.clone.lines_ref, ...), custom_call_target="tpu_custom_call" | custom-call | flops 6710886400 | bytes 12582912 | tf_op jit(solution)/shard_map/pallas_call | solution.py:242
  409.8 4.4 convolution_convert_fusion.1
  414.2 4.0 convolution_convert_fusion
  418.2 3.1 pad_maximum_fusion.2
  421.4 1.5 copy-done.30
  422.9 10.3 %convert_bitcast_fusion = bf16[1024,2048]{1,0:T(8,128)(2,1)} fusion(bf16[1024,1024]{1,0:T(8,128)(2,1)S(1)} %copy-done.30, f32[1024,2048]{1,0:T(8,128)} %fusion.35, f32[2048]{0:T(1024)S(1)} %bitcast.93), kind=kOutput, calls=%fused_computation.52 | convolution fusion | flops 4318035968 | bytes 14688256 | tf_op jit(solution)/shard_map/dot_general | solution.py:50
  433.1 10.3 %convert_bitcast_fusion.1 = bf16[1024,2048]{1,0:T(8,128)(2,1)} fusion(bf16[1024,1024]{1,0:T(8,128)(2,1)S(1)} %copy-done.30, f32[1024,2048]{1,0:T(8,128)} %fusion.42, f32[2048]{0:T(1024)S(1)} %bitcast.90), kind=kOutput, calls=%fused_computation.53 | convolution fusion | flops 4318035968 | bytes 14688256 | tf_op jit(solution)/shard_map/dot_general | solution.py:50
  443.4 8.3 pad_maximum_fusion.1
  452.0 1.3 copy-done.26
  453.4 8.4 convolution_convert_fusion.2
  461.7 6.1 convolution_convert_fusion.3
  467.8 8.3 pad_maximum_fusion
  476.9 8.6 fusion.31
  485.5 10.8 %add_convert_fusion.2 = bf16[1024,1024]{0,1:T(8,128)(2,1)} fusion(f32[1024,1024]{0,1:T(8,128)S(1)} %copy-done.16, f32[1024,1024]{0,1:T(8,128)S(1)} %fusion.31, f32[1024]{0:T(1024)S(1)} %convert_element_type.458, bf16[2048,2048]{1,0:T(8,128)(2,1)} %all-gather.12.cloned.1.call-done, f32[1024,2048]{1,0:T(8,128)} %fusion.42, f32[2048]{0:T(1024)S(1)} %bitcast.91), kind=kOutput, calls=%fused_computation.56 | convolution fusion | flops 4320133120 | bytes 23080960 | tf_op jit(solution)/shard_map/dot_general | solution.py:46
  496.3 4.3 copy.118
  500.6 5.6 fusion.44
  506.2 6.6 fusion.27
  512.9 2.7 fusion.26
  515.6 4.0 copy.119
  519.7 2.6 convert_reduce_fusion.3
  522.8 41.2 %all-reduce.2 = (f32[1024]{0:T(1024)}, f32[1024]{0:T(1024)}, f32[3072]{0:T(1024)S(1)}, f32[1024]{0:T(1024)}, f32[1024]{0:T(1024)}, /*index=5*/f32[1024]{0:T(1024)}, f32[4096]{0:T(1024)S(1)}, f32[1024]{0:T(1024)}) all-reduce(f32[1024]{0:T(1024)S(1)} %get-tuple-element.112, ...), channel_id=1, replica_groups=mesh['dp'=16,'tensor'=2] {'dp','tensor'}, use_global_device_ids=true, to_apply=%region_11.12 | all-reduce | flops 13312 | bytes 106496 | tf_op jit(solution)/shard_map/psum | solution.py:411
  565.2 1.5 convert_bitcast_fusion.4
  566.7 41.6 %reduce-scatter.5.cloned.1.call-done = bf16[64,1536]{1,0:T(8,128)(2,1)} async-done(((bf16[2048,1536]{1,0:T(8,128)(2,1)}), bf16[64,1536]{1,0:T(8,128)(2,1)}) %reduce-scatter.5.cloned.1.call-update) | async-done | bytes 196624 | tf_op jit(solution)/shard_map/reduce_scatter | solution.py:305
  608.4 1.3 reshape.564
  609.7 1.1 slice_reduce_fusion
  612.7 145.8 %reduce-scatter.11.cloned.1.call-done = bf16[64,2048]{1,0:T(8,128)(2,1)} async-done(((bf16[2048,2048]{1,0:T(8,128)(2,1)}), bf16[64,2048]{1,0:T(8,128)(2,1)}) %reduce-scatter.11.cloned.1.call-update) | async-done | bytes 262160 | tf_op jit(solution)/shard_map/reduce_scatter | solution.py:305
  758.6 1.8 convert_bitcast_fusion.2
  760.4 146.1 %reduce-scatter.9.cloned.1.call-done = bf16[64,2048]{1,0:T(8,128)(2,1)} async-done(((bf16[2048,2048]{1,0:T(8,128)(2,1)}), bf16[64,2048]{1,0:T(8,128)(2,1)}) %reduce-scatter.9.cloned.1.call-update) | async-done | bytes 262160 | tf_op jit(solution)/shard_map/reduce_scatter | solution.py:305
  906.5 1.8 convert_element_type.479
  (171 shorter events, 22.3 us)
Async XLA Ops:
  7.2 6.2 copy-start
  7.2 76.5 %all-gather.6.cloned.1.call-start = ((), (), s32[]{:S(2)}) async-start(), calls=%async_computation.4 | async-start | bytes 6488064 | tf_op jit(solution)/shard_map/all_gather | solution.py:299
  11.2 130.3 %all-gather.8.cloned.1.call-start = ((), (), s32[]{:S(2)}) async-start(), calls=%async_computation.5 | async-start | bytes 2162688 | tf_op jit(solution)/shard_map/all_gather | solution.py:299
  12.0 208.9 %all-gather.10.cloned.1.call-start = ((), (), s32[]{:S(2)}) async-start(), calls=%async_computation.6 | async-start | bytes 8650752 | tf_op jit(solution)/shard_map/all_gather | solution.py:299
  12.7 287.1 %all-gather.12.cloned.1.call-start = ((), (), s32[]{:S(2)}) async-start(), calls=%async_computation.7 | async-start | bytes 8650752 | tf_op jit(solution)/shard_map/all_gather | solution.py:299
  13.3 551.9 %reduce-scatter.7.cloned.1.call-start = ((), (), s32[]{:S(2)}) async-start(), calls=%async_computation.9 | async-start | bytes 2162688 | tf_op jit(solution)/shard_map/reduce_scatter | solution.py:305
  27.4 56.3 %copy-start.17 = (bf16[1024,1024]{0,1:T(8,128)(2,1)}, bf16[1024,1024]{0,1:T(8,128)(2,1)S(1)}, u32[]{:S(2)}) copy-start(bf16[1024,1024]{0,1:T(8,128)(2,1)S(1)} %copy.101) | copy-start | bytes 6291460
  89.5 14.3 %copy-start.6 = (bf16[1024,1536]{1,0:T(8,128)(2,1)}, bf16[1024,1536]{1,0:T(8,128)(2,1)S(1)}, u32[]{:S(2)}) copy-start(bf16[1024,1536]{1,0:T(8,128)(2,1)S(1)} %add_convert_fusion.1.qkv_ref) | copy-start | bytes 9437188
  89.5 15.7 %copy-start.18 = (bf16[1024,1024]{0,1:T(8,128)(2,1)S(1)}, bf16[1024,1024]{0,1:T(8,128)(2,1)}, u32[]{:S(2)}) copy-start(bf16[1024,1024]{0,1:T(8,128)(2,1)} %copy-done.17) | copy-start | bytes 6291460
  89.6 15.6 %copy-start.42 = (bf16[2048,1536]{1,0:T(8,128)(2,1)S(1)}, bf16[2048,1536]{1,0:T(8,128)(2,1)}, u32[]{:S(2)}) copy-start(bf16[2048,1536]{1,0:T(8,128)(2,1)} %all-gather.6.cloned.1.call-done) | copy-start | bytes 18874372
  103.9 1.3 copy-start.10
  123.5 1.7 copy-start.8
  125.2 1.4 copy-start.12
  141.6 2.7 copy-start.19
  141.6 2.7 copy-start.31
  145.8 2.0 copy-start.14
  220.9 10.8 %copy-start.25 = (bf16[1024,1024]{0,1:T(8,128)(2,1)S(1)}, bf16[1024,1024]{0,1:T(8,128)(2,1)}, u32[]{:S(2)}) copy-start(bf16[1024,1024]{0,1:T(8,128)(2,1)} %add_convert_fusion.3) | copy-start | bytes 6291460
  220.9 10.8 %copy-start.41 = (bf16[2048,2048]{1,0:T(8,128)(2,1)S(1)}, bf16[2048,2048]{1,0:T(8,128)(2,1)}, u32[]{:S(2)}) copy-start(bf16[2048,2048]{1,0:T(8,128)(2,1)} %all-gather.10.cloned.1.call-done) | copy-start | bytes 25165828
  313.4 9.9 %copy-start.45 = (bf16[1024,2048]{1,0:T(8,128)(2,1)}, bf16[1024,2048]{1,0:T(8,128)(2,1)S(1)}, u32[]{:S(2)}) copy-start(bf16[1024,2048]{1,0:T(8,128)(2,1)S(1)} %get-tuple-element.143) | copy-start | bytes 12582916
  313.4 9.9 %copy-start.29 = (bf16[1024,1024]{1,0:T(8,128)(2,1)S(1)}, bf16[1024,1024]{1,0:T(8,128)(2,1)}, u32[]{:S(2)}) copy-start(bf16[1024,1024]{1,0:T(8,128)(2,1)} %param.35) | copy-start | bytes 6291460
  313.4 9.9 %copy-start.40 = (bf16[2048,2048]{1,0:T(8,128)(2,1)S(1)}, bf16[2048,2048]{1,0:T(8,128)(2,1)}, u32[]{:S(2)}) copy-start(bf16[2048,2048]{1,0:T(8,128)(2,1)} %all-gather.12.cloned.1.call-done) | copy-start | bytes 25165828
  323.2 12.6 %copy-start.15 = (f32[1024,1024]{0,1:T(8,128)S(1)}, f32[1024,1024]{0,1:T(8,128)}, u32[]{:S(2)}) copy-start(f32[1024,1024]{0,1:T(8,128)} %copy-done.14) | copy-start | bytes 12582916
  335.8 11.0 %copy-start.43 = (bf16[1024,2048]{1,0:T(8,128)(2,1)}, bf16[1024,2048]{1,0:T(8,128)(2,1)S(1)}, u32[]{:S(2)}) copy-start(bf16[1024,2048]{1,0:T(8,128)(2,1)S(1)} %get-tuple-element.145) | copy-start | bytes 12582916
  335.8 11.0 %copy-start.24 = (bf16[1024,1024]{0,1:T(8,128)(2,1)S(1)}, bf16[1024,1024]{0,1:T(8,128)(2,1)}, u32[]{:S(2)}) copy-start(bf16[1024,1024]{0,1:T(8,128)(2,1)} %copy.112) | copy-start | bytes 6291460
  350.1 1.9 copy-start.22
  350.4 2.2 copy-start.27
  355.4 253.0 %reduce-scatter.5.cloned.1.call-start = ((), (), s32[]{:S(2)}) async-start(), calls=%async_computation.8 | async-start | bytes 6488064 | tf_op jit(solution)/shard_map/reduce_scatter | solution.py:305
  355.5 3.3 copy-start.28
  355.5 3.3 copy-start.32
  358.8 1.9 copy-start.9
  358.8 2.6 copy-start.13
  361.4 24.2 %copy-start.7 = (bf16[1024,1536]{1,0:T(8,128)(2,1)S(1)}, bf16[1024,1536]{1,0:T(8,128)(2,1)}, u32[]{:S(2)}) copy-start(bf16[1024,1536]{1,0:T(8,128)(2,1)} %copy-done.6) | copy-start | bytes 9437188
  361.4 24.2 %copy-start.11 = (f32[1024,512]{1,0:T(8,128)S(1)}, f32[1024,512]{1,0:T(8,128)}, u32[]{:S(2)}) copy-start(f32[1024,512]{1,0:T(8,128)} %copy-done.10) | copy-start | bytes 6291460
  385.6 28.6 %copy-start.2 = (bf16[1024,1536]{1,0:T(8,128)(2,1)}, bf16[1024,1536]{1,0:T(8,128)(2,1)S(1)}, u32[]{:S(2)}) copy-start(bf16[1024,1536]{1,0:T(8,128)(2,1)S(1)} %shard_map.308) | copy-start | bytes 9437188
  385.6 24.1 %copy-start.20 = (bf16[1024,1024]{0,1:T(8,128)(2,1)S(1)}, bf16[1024,1024]{0,1:T(8,128)(2,1)}, u32[]{:S(2)}) copy-start(bf16[1024,1024]{0,1:T(8,128)(2,1)} %copy-done.17) | copy-start | bytes 6291460
  409.7 4.4 copy-start.4
  421.3 1.6 copy-start.30
  421.3 337.3 %reduce-scatter.11.cloned.1.call-start = ((), (), s32[]{:S(2)}) async-start(), calls=%async_computation.11 | async-start | bytes 8650752 | tf_op jit(solution)/shard_map/reduce_scatter | solution.py:305
  451.8 1.6 copy-start.26
  451.8 454.7 %reduce-scatter.9.cloned.1.call-start = ((), (), s32[]{:S(2)}) async-start(), calls=%async_computation.10 | async-start | bytes 8650752 | tf_op jit(solution)/shard_map/reduce_scatter | solution.py:305
  453.4 8.4 copy-start.44
  476.2 0.7 copy-start.39
  476.9 8.6 copy-start.16
  496.3 4.3 copy-start.3
  500.6 5.6 copy-start.5
  500.6 5.6 copy-start.21
  506.2 6.7 copy-start.23
  519.6 3.1 copy-start.35
  519.6 3.1 copy-start.36
  519.6 3.1 copy-start.33
  519.6 3.2 copy-start.34
  519.6 3.2 copy-start.37
  519.6 3.2 copy-start.38
  519.6 388.6 %copy-start.1 = (s32[2,4]{1,0:T(2,128)S(1)}, s32[2,4]{1,0:T(2,128)}, u32[]{:S(2)}) copy-start(s32[2,4]{1,0:T(2,128)} %param.19) | copy-start | bytes 100
Sparse Core Ops, SparseCore 0:
  11.5 72.1 all-gather.5
  86.6 54.9 all-gather.7
  144.5 76.4 all-gather.9
  223.6 76.1 all-gather.11
  355.5 135.4 reduce-scatter.6
  497.5 110.8 reduce-scatter.4
  610.7 147.8 reduce-scatter.10
  760.9 145.5 reduce-scatter.8
